TPU v7x, 32 devices: a whole 2x2x4 slice. The times are simulated.
32 devices in a mesh: grp: 2 (over x), row: 8 (over z, y), col: 2 (over core).
Axes of the slice: x: 2, y: 2, z: 4, core: 2. Of those that a mesh axis runs over, the one named last changes fastest.
Arguments:
- alignment_activations: bfloat16 [2, 64, 128, 256], P(None, ('grp', 'row')), parts along dimension 1, may hold values from -6 to 6
- first_projection_matrix: bfloat16 [2, 256, 32], replicated, may hold values from -0.375 to 0.375
- second_projection_matrix: bfloat16 [2, 256, 32], replicated, may hold values from -0.375 to 0.375
- final_projection_matrix: bfloat16 [2, 1024, 128], replicated, may hold values from -1 to 1
- final_offset_vector: float32 [2, 128], replicated, may hold values from -3 to 3
Outputs:
- update: bfloat16 [2, 256, 128, 128], P(None, ('grp', 'row'), 'col'), parts along dimension 1
There are 2 independent parts, one for each index of `grp`. A program takes and returns all parts, laid end to end along the dimension named above; an argument that names none is the same for every part. Nothing has to cross between parts.
All inputs are finite; a program needn't handle non-finite values.
Results may differ from a plain program's by a relative error of at most 0.007.
Values may be sent and summed in bfloat16 or wider, within the bound.
A program may use at most 128 MiB of HBM per device.

v0:
```python
import jax
import jax.numpy as jnp
from jax import lax
from jax.sharding import PartitionSpec as P


def standardize_features(activations):
    entry_lines = activations.astype(jnp.float32)
    average = jnp.mean(entry_lines, axis=-1, keepdims=True)
    centred = entry_lines - average
    variance = jnp.mean(centred * centred, axis=-1, keepdims=True)
    return (centred * lax.rsqrt(variance + 1e-05)).astype(jnp.bfloat16)


def pair_tiles(left_tile, right_tile, final_matrix, offset_vector):
    depth_all = left_tile.shape[0]
    tile_rows = left_tile.shape[1]
    tile_cols = right_tile.shape[1]
    hidden = left_tile.shape[2]
    pair_width = final_matrix.shape[1]
    block_rows = max(1, min(tile_rows, 2048 // tile_cols))
    reciprocal = 1.0 / depth_all

    def tile_block(offset):
        left_block = lax.dynamic_slice_in_dim(left_tile, offset, block_rows, 1)
        products = (
            jnp.einsum("sic,sjd->ijcd", left_block, right_tile, preferred_element_type=jnp.float32)
            * reciprocal
        )
        products = products.astype(jnp.bfloat16).reshape(block_rows * tile_cols, hidden * hidden)
        projected = (
            jnp.dot(products, final_matrix, preferred_element_type=jnp.float32) + offset_vector
        )
        return projected.astype(jnp.bfloat16).reshape(block_rows, tile_cols, pair_width)

    starts = jnp.arange(tile_rows // block_rows, dtype=jnp.int32) * block_rows
    return lax.map(tile_block, starts).reshape(tile_rows, tile_cols, pair_width)


def block_update(activations, first_matrix, second_matrix, final_matrix, offset_vector):
    local_sequences, sequence_positions, feature_number = activations.shape
    row_count = lax.axis_size("row")
    col_count = lax.axis_size("col")
    row_block = sequence_positions // row_count
    col_block = sequence_positions // col_count
    hidden = first_matrix.shape[1]
    unrolled_products = standardize_features(activations).reshape(
        local_sequences * sequence_positions, feature_number
    )
    first_factor = jnp.dot(
        unrolled_products, first_matrix, preferred_element_type=jnp.float32
    ).astype(jnp.bfloat16)
    second_factor = jnp.dot(
        unrolled_products, second_matrix, preferred_element_type=jnp.float32
    ).astype(jnp.bfloat16)
    col_place = lax.axis_index("col")
    halves = second_factor.reshape(local_sequences, col_count, col_block * hidden)
    own_half = lax.dynamic_index_in_dim(halves, col_place, 1, keepdims=False)
    left_send = first_factor.reshape(local_sequences, row_count, row_block * hidden)
    left_got = lax.all_to_all(left_send, "row", split_axis=1, concat_axis=0, tiled=True)
    left_tile = left_got.reshape(-1, row_block, hidden)
    panel = lax.all_gather(own_half, "row", axis=0, tiled=True)
    right_tile = panel.reshape(-1, col_block, hidden)
    return pair_tiles(left_tile, right_tile, final_matrix, offset_vector)


def body(
    alignment_activations,
    first_projection_matrix,
    second_projection_matrix,
    final_projection_matrix,
    final_offset_vector,
):
    results = []
    for layer in range(alignment_activations.shape[0]):
        results.append(
            block_update(
                alignment_activations[layer],
                first_projection_matrix[layer],
                second_projection_matrix[layer],
                final_projection_matrix[layer],
                final_offset_vector[layer],
            )
        )
    return jnp.stack(results, axis=0)


def solution(mesh):
    in_specs = (P(None, ("grp", "row"), None, None), P(), P(), P(), P())
    out_specs = P(None, ("grp", "row"), "col", None)
    return jax.shard_map(body, mesh=mesh, in_specs=in_specs, out_specs=out_specs, check_vma=False)
```

profile of v0, /device:TPU:0, one launch (start us, length us, event | category | flops | bytes accessed | tf_op | source)
XLA Modules:
  0.0 113.5 jit_solution(3730339514740739942)
XLA Ops:
  0.0 1.3 %convert_reduce_fusion.1 = (f32[4,128]{1,0:T(4,128)S(1)}, f32[4,128]{1,0:T(4,128)S(1)}) fusion(bf16[2,4,128,256]{3,2,1,0:T(8,128)(2,1)} %param.5), kind=kLoop, calls=%fused_computation.17 | loop fusion | flops 523264 | bytes 528384 | tf_op jit(solution)/shard_map/reduce_sum | solution.py:9
  1.3 1.4 %fusion.8 = (f32[4,128]{1,0:T(4,128)S(1)}, f32[4,128]{1,0:T(4,128)S(1)}) fusion(f32[4,128]{1,0:T(4,128)S(1)} %get-tuple-element.48, bf16[2,4,128,256]{3,2,1,0:T(8,128)(2,1)} %param.5, f32[4,128]{1,0:T(4,128)S(1)} %get-tuple-element.41), kind=kLoop, calls=%fused_computation.22 | loop fusion | flops 1047552 | bytes 532480 | tf_op jit(solution)/shard_map/reduce_sum | solution.py:11
  2.7 1.4 %fusion.5 = (bf16[1,4,128,256]{3,2,1,0:T(8,128)(2,1)S(1)}, bf16[1,4,128,256]{3,2,1,0:T(8,128)(2,1)S(1)}) fusion(f32[4,128]{1,0:T(4,128)S(1)} %add_rsqrt_fusion.1, f32[4,128]{1,0:T(4,128)S(1)} %get-tuple-element.48, bf16[2,4,128,256]{3,2,1,0:T(8,128)(2,1)} %param.5, f32[4,128]{1,0:T(4,128)S(1)} %add_rsqrt_fusion, f32[4,128]{1,0:T(4,128)S(1)} %get-tuple-element.41), kind=kLoop, calls=%fused_computation.19 | loop fusion | flops 1048576 | bytes 1056768 | tf_op jit(solution)/shard_map/convert_element_type | solution.py:12
  4.1 0.9 convolution_convert_fusion.2
  5.9 7.3 %all-to-all-start = ((bf16[4,8,512]{2,0,1:T(4,128)(2,1)}), bf16[4,8,512]{2,0,1:T(4,128)(2,1)S(1)}, u32[]{:S(2)}, u32[]{:S(2)}) async-start(bf16[4,8,512]{2,0,1:T(4,128)(2,1)} %copy.20), calls=%async_computation | async-start | bytes 65536 | tf_op jit(solution)/shard_map/all_to_all | solution.py:60
  13.2 0.9 convolution_convert_fusion.3
  14.1 0.9 convolution_convert_fusion.1
  15.0 0.9 convolution_convert_fusion
  16.2 31.3 %all-gather = bf16[32,1,2048]{2,1,0:T(2,128)(2,1)S(1)} all-gather(bf16[4,1,2048]{2,1,0:T(2,128)(2,1)S(1)} %constant_dynamic-slice_fusion.1), channel_id=2, replica_groups=mesh['grp'=2,'row'=8,'col'=2] {'row'}, dimensions={0}, use_global_device_ids=true | all-gather | bytes 147456 | tf_op jit(solution)/shard_map/all_gather | solution.py:62
  47.5 0.7 reduce.2
  49.5 30.9 %all-gather.1 = bf16[32,1,2048]{2,1,0:T(2,128)(2,1)S(1)} all-gather(bf16[4,1,2048]{2,1,0:T(2,128)(2,1)S(1)} %constant_dynamic-slice_fusion), channel_id=3, replica_groups=mesh['grp'=2,'row'=8,'col'=2] {'row'}, dimensions={0}, use_global_device_ids=true | all-gather | bytes 147456 | tf_op jit(solution)/shard_map/all_gather | solution.py:62
  80.3 0.7 reduce.3
  82.2 0.6 copy.26
  82.8 5.3 %all-to-all-start.1 = ((bf16[4,8,512]{2,0,1:T(4,128)(2,1)}), bf16[4,8,512]{2,0,1:T(4,128)(2,1)S(1)}, u32[]{:S(2)}, u32[]{:S(2)}) async-start(bf16[4,8,512]{2,0,1:T(4,128)(2,1)} %copy.26), calls=%async_computation.1 | async-start | bytes 65536 | tf_op jit(solution)/shard_map/all_to_all | solution.py:60
  88.4 1.2 %fusion = bf16[16,64,32,32]{1,2,0,3:T(8,128)(2,1)S(1)} fusion(bf16[32,64,32,1]{1,0,3,2:T(8,128)(2,1)S(1)} %copy.30, bf16[32,16,32]{0,2,1:T(8,128)(2,1)S(1)} %copy.22), kind=kOutput, calls=%fused_computation.2 | convolution fusion | flops 69206016 | bytes 2260992 | tf_op jit(solution)/shard_map/while/body/eval_jaxpr/sic,sjd->ijcd/dot_general | solution.py:27
  89.7 3.5 %copy.23 = bf16[16,64,32,32]{1,0,3,2:T(8,128)(2,1)} copy(bf16[16,64,32,32]{1,2,0,3:T(8,128)(2,1)S(1)} %fusion) | data formatting | bytes 4194304 | tf_op jit(solution)/shard_map/while/body/eval_jaxpr/convert_element_type | solution.py:30
  93.2 5.5 %reshape.142 = bf16[1024,1024]{0,1:T(8,128)(2,1)S(1)} reshape(bf16[16,64,32,32]{1,0,3,2:T(8,128)(2,1)} %copy.23) | data formatting | bytes 4194304 | tf_op jit(solution)/shard_map/while/body/eval_jaxpr/reshape | solution.py:30
  99.0 1.2 %fusion.1 = bf16[16,64,32,32]{1,2,0,3:T(8,128)(2,1)S(1)} fusion(bf16[32,64,32,1]{1,0,3,2:T(8,128)(2,1)S(1)} %copy.31, bf16[32,16,32]{0,2,1:T(8,128)(2,1)S(1)} %copy.28), kind=kOutput, calls=%fused_computation.3 | convolution fusion | flops 69206016 | bytes 2260992 | tf_op jit(solution)/shard_map/while/body/eval_jaxpr/sic,sjd->ijcd/dot_general | solution.py:27
  100.2 3.5 %copy.29 = bf16[16,64,32,32]{1,0,3,2:T(8,128)(2,1)} copy(bf16[16,64,32,32]{1,2,0,3:T(8,128)(2,1)S(1)} %fusion.1) | data formatting | bytes 4194304 | tf_op jit(solution)/shard_map/while/body/eval_jaxpr/convert_element_type | solution.py:30
  103.8 6.6 %reshape.147 = bf16[1024,1024]{0,1:T(8,128)(2,1)} reshape(bf16[16,64,32,32]{1,0,3,2:T(8,128)(2,1)} %copy.29) | data formatting | bytes 4194304 | tf_op jit(solution)/shard_map/while/body/eval_jaxpr/reshape | solution.py:30
  110.4 0.7 fusion.2
  111.1 0.8 copy-done
  111.9 0.7 fusion.3
  112.7 0.8 pad_maximum_fusion
  (30 shorter events, 4.1 us)
Async XLA Ops:
  0.0 49.1 %copy-start.1 = (f32[2,128]{1,0:T(2,128)S(1)}, f32[2,128]{1,0:T(2,128)}, u32[]{:S(2)}) copy-start(f32[2,128]{1,0:T(2,128)} %param.9) | copy-start | bytes 3076
  5.9 76.9 %all-to-all-start = ((bf16[4,8,512]{2,0,1:T(4,128)(2,1)}), bf16[4,8,512]{2,0,1:T(4,128)(2,1)S(1)}, u32[]{:S(2)}, u32[]{:S(2)}) async-start(bf16[4,8,512]{2,0,1:T(4,128)(2,1)} %copy.20), calls=%async_computation | async-start | bytes 65536 | tf_op jit(solution)/shard_map/all_to_all | solution.py:60
  82.8 15.9 %all-to-all-start.1 = ((bf16[4,8,512]{2,0,1:T(4,128)(2,1)}), bf16[4,8,512]{2,0,1:T(4,128)(2,1)S(1)}, u32[]{:S(2)}, u32[]{:S(2)}) async-start(bf16[4,8,512]{2,0,1:T(4,128)(2,1)} %copy.26), calls=%async_computation.1 | async-start | bytes 65536 | tf_op jit(solution)/shard_map/all_to_all | solution.py:60
  103.8 6.6 %copy-start.2 = (bf16[2,1024,128]{2,1,0:T(8,128)(2,1)S(1)}, bf16[2,1024,128]{2,1,0:T(8,128)(2,1)}, u32[]{:S(2)}) copy-start(bf16[2,1024,128]{2,1,0:T(8,128)(2,1)} %param.8) | copy-start | bytes 1572868
  110.4 1.6 %copy-start = (bf16[1024,1024]{0,1:T(8,128)(2,1)S(1)}, bf16[1024,1024]{0,1:T(8,128)(2,1)}, u32[]{:S(2)}) copy-start(bf16[1024,1024]{0,1:T(8,128)(2,1)} %reshape.147) | copy-start | bytes 6291460
where the time goes:
time: 114 us
  blocking collectives  62.2 us (55%)
  local copies, waits for them, and re-layouts  24.7 us (22%)
  starting transfers between devices  12.6 us (11%)
  matrix products  7.5 us (7%)
  other arithmetic  6.35 us (6%)
    all_gather x2, blocking collectives, block_update(): panel = lax.all_gather(own_half, 'row', axis=0, tiled=True)  62.2 us
    all_to_all x2, starting transfers between devices, block_update(): lax.all_to_all(left_send, 'row', split_axis=1, concat_axis=0, tiled=True)  12.6 us
    reshape x2, local copies, waits for them, and re-layouts, tile_block(): products.astype(jnp.bfloat16)  12 us
    convert_element_type x2, local copies, waits for them, and re-layouts, tile_block(): products.astype(jnp.bfloat16)  7.09 us
    dot_general x2, matrix products, tile_block(): jnp.einsum('sic,sjd->ijcd', left_block, right_tile, preferred_element_typ...  2.44 us
  transfers between devices with their start and end apart: 2, of which 0 were waited for; matrix products, arithmetic and copies ran while one was open for 16% of the time, Pallas kernels for 0%

commit v1 on v0

--- a/solution.py
+++ b/solution.py
@@ -1,7 +1,14 @@
+import functools
+
 import jax
 import jax.numpy as jnp
 from jax import lax
+from jax.experimental import pallas as pl
+from jax.experimental.pallas import tpu as pltpu
 from jax.sharding import PartitionSpec as P
+
+LANES = 128
+VMEM_BUDGET = 48 * 1024 * 1024
 
 
 def standardize_features(activations):
@@ -64,28 +71,278 @@
     return pair_tiles(left_tile, right_tile, final_matrix, offset_vector)
 
 
-def body(
-    alignment_activations,
-    first_projection_matrix,
-    second_projection_matrix,
-    final_projection_matrix,
-    final_offset_vector,
-):
+def collective_body(activations, first_matrix, second_matrix, final_matrix, offsets):
     results = []
-    for layer in range(alignment_activations.shape[0]):
+    for layer in range(activations.shape[0]):
         results.append(
             block_update(
-                alignment_activations[layer],
-                first_projection_matrix[layer],
-                second_projection_matrix[layer],
-                final_projection_matrix[layer],
-                final_offset_vector[layer],
+                activations[layer],
+                first_matrix[layer],
+                second_matrix[layer],
+                final_matrix[layer],
+                offsets[layer],
             )
         )
     return jnp.stack(results, axis=0)
 
 
+def dot32(a, b):
+    return jnp.dot(a, b, preferred_element_type=jnp.float32)
+
+
+def dot32_nt(a, b):
+    return lax.dot_general(a, b, (((1,), (1,)), ((), ())), preferred_element_type=jnp.float32)
+
+
+def opm_kernel(
+    n,
+    x_hbm,
+    w1_ref,
+    w2_ref,
+    wf_hbm,
+    b_ref,
+    out_hbm,
+    x_ref,
+    wf_ref,
+    normed,
+    left_send,
+    right_send,
+    left_got,
+    right_got,
+    wide,
+    w_rows,
+    left_rows,
+    right_rows,
+    half_done,
+    out_ref,
+    in_sem,
+    out_sem,
+    left_ssem,
+    left_rsem,
+    right_ssem,
+    right_rsem,
+):
+    layers, seqs, positions, _ = x_ref.shape
+    hidden = w1_ref.shape[2]
+    row_block, col_block = out_ref.shape[1], out_ref.shape[2]
+    depth = n * seqs
+    pairs = seqs // 2
+    me = lax.axis_index("row")
+    col = lax.axis_index("col")
+
+    fetches = []
+    for layer in range(layers):
+        fetches.append(pltpu.make_async_copy(x_hbm.at[layer], x_ref.at[layer], in_sem.at[layer]))
+    fetches.append(pltpu.make_async_copy(wf_hbm, wf_ref, in_sem.at[layers]))
+    for fetch in fetches:
+        fetch.start()
+
+    barrier = pltpu.get_barrier_semaphore()
+    for step in range(1, n):
+        pl.semaphore_signal(
+            barrier,
+            inc=1,
+            device_id={"row": lax.rem(me + step, n)},
+            device_id_type=pl.DeviceIdType.MESH,
+        )
+
+    spread = (
+        lax.broadcasted_iota(jnp.int32, (hidden, LANES), 1) % hidden
+        == lax.broadcasted_iota(jnp.int32, (hidden, LANES), 0)
+    ).astype(jnp.bfloat16)
+    same = (
+        lax.broadcasted_iota(jnp.int32, (hidden, hidden), 1)
+        == lax.broadcasted_iota(jnp.int32, (hidden, hidden), 0)
+    ).astype(jnp.bfloat16)
+
+    copies = []
+    for layer in range(layers):
+        fetches[layer].wait()
+        w1_wide = dot32(w1_ref[layer], spread).astype(jnp.bfloat16)
+        w2_turned = dot32_nt(same, w2_ref[layer]).astype(jnp.bfloat16)
+        lane = lax.broadcasted_iota(jnp.int32, (positions, LANES), 1)
+        packed = jnp.zeros((positions, LANES), jnp.float32)
+        for s in range(seqs):
+            entry = standardize_features(x_ref[layer, s])
+            normed[s] = entry
+            group = (lane >= s * hidden) & (lane < (s + 1) * hidden)
+            packed = jnp.where(group, dot32(entry, w1_wide), packed)
+        left_send[layer] = packed.astype(jnp.bfloat16)
+        mine = pl.ds(pl.multiple_of(col * col_block, col_block), col_block)
+        for low in range(pairs):
+            both = jnp.concatenate([normed[low, mine, :], normed[low + pairs, mine, :]], axis=0)
+            right = dot32_nt(w2_turned, both).astype(jnp.bfloat16)
+            right_send[layer, low * hidden : (low + 1) * hidden, :] = right
+        own_rows = pl.ds(pl.multiple_of(me * row_block, row_block), row_block)
+        left_got[layer, me] = left_send[layer, own_rows, :]
+        right_got[layer, me] = right_send[layer]
+        if layer == 0:
+            pl.semaphore_wait(barrier, n - 1)
+        for step in range(1, n):
+            to = lax.rem(me + step, n)
+            their_rows = pl.ds(pl.multiple_of(to * row_block, row_block), row_block)
+            left_copy = pltpu.make_async_remote_copy(
+                src_ref=left_send.at[layer, their_rows, :],
+                dst_ref=left_got.at[layer, me],
+                send_sem=left_ssem.at[layer, step],
+                recv_sem=left_rsem.at[layer, me],
+                device_id={"row": to},
+                device_id_type=pl.DeviceIdType.MESH,
+            )
+            right_copy = pltpu.make_async_remote_copy(
+                src_ref=right_send.at[layer],
+                dst_ref=right_got.at[layer, me],
+                send_sem=right_ssem.at[layer, step],
+                recv_sem=right_rsem.at[layer, me],
+                device_id={"row": to},
+                device_id_type=pl.DeviceIdType.MESH,
+            )
+            left_copy.start()
+            right_copy.start()
+            copies.extend([left_copy, right_copy])
+
+    fetches[layers].wait()
+    for layer in range(layers):
+        wide[...] = wf_ref[layer].astype(jnp.float32)
+        for d in range(hidden):
+            piece = wide[pl.ds(d, hidden, stride=hidden), :].astype(jnp.bfloat16)
+            for s in range(seqs):
+                w_rows[layer, s * hidden : (s + 1) * hidden, d * LANES : (d + 1) * LANES] = piece
+
+    lane = lax.broadcasted_iota(jnp.int32, (row_block, LANES), 1)
+    stores = []
+    for layer in range(layers):
+        for step in range(1, n):
+            source = lax.rem(me + n - step, n)
+            pltpu.make_async_remote_copy(
+                src_ref=left_got.at[layer, source],
+                dst_ref=left_got.at[layer, source],
+                send_sem=left_ssem.at[layer, step],
+                recv_sem=left_rsem.at[layer, source],
+                device_id={"row": source},
+                device_id_type=pl.DeviceIdType.MESH,
+            ).wait_recv()
+        for r in range(n):
+            block = left_got[layer, r].astype(jnp.float32)
+            for s in range(seqs):
+                group = (lane >= s * hidden) & (lane < (s + 1) * hidden)
+                left_rows[pl.ds(r * seqs + s, row_block, stride=depth), :] = jnp.where(
+                    group, block, 0.0
+                )
+        left_all = left_rows[...].astype(jnp.bfloat16)
+        for d in range(0, hidden, 2):
+            two = dot32(left_all, w_rows[layer, :, d * LANES : (d + 2) * LANES])
+            two = two.astype(jnp.bfloat16)
+            for k in range(2):
+                for i in range(row_block):
+                    half_done[
+                        (d + k) * depth : (d + k + 1) * depth, i * LANES : (i + 1) * LANES
+                    ] = two[i * depth : (i + 1) * depth, k * LANES : (k + 1) * LANES]
+
+        for step in range(1, n):
+            source = lax.rem(me + n - step, n)
+            pltpu.make_async_remote_copy(
+                src_ref=right_got.at[layer, source],
+                dst_ref=right_got.at[layer, source],
+                send_sem=right_ssem.at[layer, step],
+                recv_sem=right_rsem.at[layer, source],
+                device_id={"row": source},
+                device_id_type=pl.DeviceIdType.MESH,
+            ).wait_recv()
+        for r in range(n):
+            for low in range(pairs):
+                block = right_got[layer, r, low * hidden : (low + 1) * hidden, :]
+                block = block.astype(jnp.float32)
+                right_rows[pl.ds(r * seqs + low, hidden, stride=depth), :] = block
+                right_rows[pl.ds(r * seqs + low + pairs, hidden, stride=depth), :] = pltpu.roll(
+                    block, col_block, 1
+                )
+        right_all = right_rows[...].T[:col_block].astype(jnp.bfloat16)
+        scale = 1.0 / depth
+        for i in range(0, row_block, 2):
+            two = dot32(right_all, half_done[:, i * LANES : (i + 2) * LANES]) * scale
+            for k in range(2):
+                done = two[:, k * LANES : (k + 1) * LANES] + b_ref[layer : layer + 1, :]
+                out_ref[layer, i + k] = done.astype(jnp.bfloat16)
+        store = pltpu.make_async_copy(out_ref.at[layer], out_hbm.at[layer], out_sem.at[layer])
+        store.start()
+        stores.append(store)
+
+    for copy in copies:
+        copy.wait_send()
+    for store in stores:
+        store.wait()
+
+
+def kernel_fits(n, cols, x_shape, hidden, pair_width):
+    layers, seqs, positions, features = x_shape
+    row_block, col_block = positions // n, positions // cols
+    depth = n * seqs
+    need = 4 * layers * seqs * positions * features + 4 * depth * hidden * row_block * pair_width
+    return (
+        seqs * hidden == LANES
+        and seqs % 2 == 0
+        and 2 * col_block == LANES
+        and pair_width == LANES
+        and row_block % 16 == 0
+        and depth % 16 == 0
+        and n > 1
+        and need < VMEM_BUDGET
+    )
+
+
+def kernel_body(n, cols, x, w1, w2, wf, b):
+    layers, seqs, positions, features = x.shape
+    hidden = w1.shape[2]
+    pair_width = wf.shape[2]
+    row_block, col_block = positions // n, positions // cols
+    depth = n * seqs
+    packed = (seqs // 2) * hidden
+    bf16, f32 = jnp.bfloat16, jnp.float32
+    vmem = pl.BlockSpec(memory_space=pltpu.VMEM)
+    anywhere = pl.BlockSpec(memory_space=pl.ANY)
+    out_shape = (layers, row_block, col_block, pair_width)
+    return pl.pallas_call(
+        functools.partial(opm_kernel, n),
+        out_shape=jax.ShapeDtypeStruct(out_shape, bf16),
+        in_specs=[anywhere, vmem, vmem, anywhere, vmem],
+        out_specs=anywhere,
+        scratch_shapes=[
+            pltpu.VMEM(x.shape, bf16),
+            pltpu.VMEM(wf.shape, bf16),
+            pltpu.VMEM((seqs, positions, features), bf16),
+            pltpu.VMEM((layers, positions, LANES), bf16),
+            pltpu.VMEM((layers, packed, LANES), bf16),
+            pltpu.VMEM((layers, n, row_block, LANES), bf16),
+            pltpu.VMEM((layers, n, packed, LANES), bf16),
+            pltpu.VMEM((hidden * hidden, pair_width), f32),
+            pltpu.VMEM((layers, LANES, hidden * pair_width), bf16),
+            pltpu.VMEM((row_block * depth, LANES), f32),
+            pltpu.VMEM((hidden * depth, LANES), f32),
+            pltpu.VMEM((hidden * depth, row_block * pair_width), bf16),
+            pltpu.VMEM(out_shape, bf16),
+            pltpu.SemaphoreType.DMA((layers + 1,)),
+            pltpu.SemaphoreType.DMA((layers,)),
+            pltpu.SemaphoreType.DMA((layers, n)),
+            pltpu.SemaphoreType.DMA((layers, n)),
+            pltpu.SemaphoreType.DMA((layers, n)),
+            pltpu.SemaphoreType.DMA((layers, n)),
+        ],
+        compiler_params=pltpu.CompilerParams(
+            collective_id=0, has_side_effects=True, vmem_limit_bytes=VMEM_BUDGET
+        ),
+        name="outer_product_mean",
+    )(x, w1, w2, wf, b)
+
+
 def solution(mesh):
+    n, cols = mesh.shape["row"], mesh.shape["col"]
+
+    def body(x, w1, w2, wf, b):
+        if kernel_fits(n, cols, x.shape, w1.shape[2], wf.shape[2]):
+            return kernel_body(n, cols, x, w1, w2, wf, b)
+        return collective_body(x, w1, w2, wf, b)
+
     in_specs = (P(None, ("grp", "row"), None, None), P(), P(), P(), P())
     out_specs = P(None, ("grp", "row"), "col", None)
     return jax.shard_map(body, mesh=mesh, in_specs=in_specs, out_specs=out_specs, check_vma=False)

time: 114 us -> 20.9 us (0.18)
  blocking collectives: 62.2 us -> 0 us
  local copies, waits for them, and re-layouts: 24.7 us -> 4.44 us
  Pallas kernels: 0 us -> 16.1 us
  starting transfers between devices: 12.6 us -> 0 us
  matrix products: 7.5 us -> 0 us
  other arithmetic: 6.35 us -> 0 us
    all_gather x2 -> x0, blocking collectives: 62.2 us -> none  [block_update(): panel = lax.all_gather(own_half, 'row', axis=0, tiled=True)]
    reshape x16 -> x0, local copies, waits for them, and re-layouts: 16.1 us -> none  [the longest x2 12 us: tile_block(): products.astype(jnp.bfloat16)]
    pallas_call x0 -> x1, Pallas kernels: none -> 16.1 us  [kernel_body(): pl.pallas_call(functools.partial(opm_kernel, n), out_shape=jax.ShapeDtype...]
    all_to_all x2 -> x0, starting transfers between devices: 12.6 us -> none  [block_update(): lax.all_to_all(left_send, 'row', split_axis=1, concat_axis=0, tiled=True)]
    convert_element_type x6 -> x0, local copies, waits for them, and re-layouts: 7.61 us -> none  [the longest x2 7.09 us: tile_block(): products.astype(jnp.bfloat16)]
    dot_general x8 -> x0, matrix products: 7.5 us -> none  [the longest x2 2.44 us: tile_block(): jnp.einsum('sic,sjd->ijcd', left_block, right_tile, preferred_element_typ...]
    unnamed x6 -> x11, local copies, waits for them, and re-layouts: 0.85 us -> 4.44 us
    reduce_sum x2 -> x0, other arithmetic: 2.66 us -> none  [the longest x1 1.41 us: standardize_features(): variance = jnp.mean(centred * centred, axis=-1, keepdims=True)]
  transfers between devices with their start and end apart: 2 -> 0, of which waited for: 0 -> 0; matrix products, arithmetic and copies ran while one was open for 16% -> 0% of each run, Pallas kernels for 0% -> 0%
where the time goes in v1:
time: 20.9 us; the launch traced here: 20.6 us
  Pallas kernels  16.1 us (77%)
  local copies, waits for them, and re-layouts  4.44 us (21%)
    pallas_call x1, Pallas kernels, kernel_body(): pl.pallas_call(functools.partial(opm_kernel, n), out_shape=jax.ShapeDtype...  16.1 us
    unnamed x11, local copies, waits for them, and re-layouts  4.44 us

profile of v1, /device:TPU:0, one launch (start us, length us, event | category | flops | bytes accessed | tf_op | source)
XLA Modules:
  0.0 20.6 jit_solution(8885919180865609472)
XLA Ops:
  0.0 0.0 copy-start.3
  0.0 0.9 %copy.6.w1_ref = bf16[2,256,32]{2,1,0:T(8,128)(2,1)S(1)} copy(bf16[2,256,32]{1,2,0:T(8,128)(2,1)} %param.6) | data formatting | bytes 65536 | tf_op args[1]
  0.9 0.0 copy-done.3
  0.9 0.0 copy-start.2
  0.9 0.1 copy.7.w2_ref
  1.0 0.5 %copy-done.2 = f32[2,128]{1,0:T(2,128)S(1)} copy-done((f32[2,128]{1,0:T(2,128)S(1)}, f32[2,128]{1,0:T(2,128)}, u32[]{:S(2)}) %copy-start.2) | copy-done | bytes 1048
  1.6 0.0 copy-start
  1.6 1.0 %copy-done = bf16[2,4,128,256]{3,2,1,0:T(8,128)(2,1)S(1)} copy-done((bf16[2,4,128,256]{3,2,1,0:T(8,128)(2,1)S(1)}, bf16[2,4,128,256]{3,2,1,0:T(8,128)(2,1)}, u32[]{:S(2)}) %copy-start) | copy-done | bytes 524312
  2.6 0.0 copy-start.1
  2.6 1.0 %copy-done.1 = bf16[2,1024,128]{2,1,0:T(8,128)(2,1)S(1)} copy-done((bf16[2,1024,128]{2,1,0:T(8,128)(2,1)S(1)}, bf16[2,1024,128]{2,1,0:T(8,128)(2,1)}, u32[]{:S(2)}) %copy-start.1) | copy-done | bytes 524312
  3.7 16.1 %outer_product_mean.1 = bf16[2,16,64,128]{3,2,1,0:T(8,128)(2,1)S(1)} custom-call(bf16[2,4,128,256]{3,2,1,0:T(8,128)(2,1)S(1)} %copy-done, bf16[2,256,32]{2,1,0:T(8,128)(2,1)S(1)} %copy.6.w1_ref, bf16[2,256,32]{2,1,0:T(8,128)(2,1)S(1)} %copy.7.w2_ref, bf16[2,1024,128]{2,1,0:T(8,128)(2,1)S(1)} %copy-done.1, f32[2,128]{1,0:T(2,128)S(1)} %copy-done.2), custom_call_target="tpu_custom_call" | custom-call | tf_op jit(solution)/shard_map/outer_product_mean/pallas_call | solution.py:305
  19.8 0.8 %copy.9 = bf16[2,16,64,128]{3,2,1,0:T(8,128)(2,1)} copy(bf16[2,16,64,128]{3,2,1,0:T(8,128)(2,1)S(1)} %outer_product_mean.1) | data formatting | bytes 1048576
Async XLA Ops:
  0.0 0.9 %copy-start.3 = (bf16[2,256,32]{1,2,0:T(8,128)(2,1)S(1)}, bf16[2,256,32]{1,2,0:T(8,128)(2,1)}, u32[]{:S(2)}) copy-start(bf16[2,256,32]{1,2,0:T(8,128)(2,1)} %param.7) | copy-start | bytes 98308
  0.9 0.7 %copy-start.2 = (f32[2,128]{1,0:T(2,128)S(1)}, f32[2,128]{1,0:T(2,128)}, u32[]{:S(2)}) copy-start(f32[2,128]{1,0:T(2,128)} %b_ref.1) | copy-start | bytes 3076
  1.6 1.0 %copy-start = (bf16[2,4,128,256]{3,2,1,0:T(8,128)(2,1)S(1)}, bf16[2,4,128,256]{3,2,1,0:T(8,128)(2,1)}, u32[]{:S(2)}) copy-start(bf16[2,4,128,256]{3,2,1,0:T(8,128)(2,1)} %x_hbm.1) | copy-start | bytes 1572868
  2.6 1.0 %copy-start.1 = (bf16[2,1024,128]{2,1,0:T(8,128)(2,1)S(1)}, bf16[2,1024,128]{2,1,0:T(8,128)(2,1)}, u32[]{:S(2)}) copy-start(bf16[2,1024,128]{2,1,0:T(8,128)(2,1)} %wf_hbm.1) | copy-start | bytes 1572868

commit v2 on v1

--- a/solution.py
+++ b/solution.py
@@ -8,7 +8,7 @@
 from jax.sharding import PartitionSpec as P
 
 LANES = 128
-VMEM_BUDGET = 48 * 1024 * 1024
+VMEM_BUDGET = 63 * 1024 * 1024
 
 
 def standardize_features(activations):
@@ -97,13 +97,16 @@
 def opm_kernel(
     n,
     x_hbm,
+    w1_hbm,
+    w2_hbm,
+    wf_hbm,
+    b_hbm,
+    out_hbm,
+    x_ref,
     w1_ref,
     w2_ref,
-    wf_hbm,
+    wf_ref,
     b_ref,
-    out_hbm,
-    x_ref,
-    wf_ref,
     normed,
     left_send,
     right_send,
@@ -123,19 +126,12 @@
     right_rsem,
 ):
     layers, seqs, positions, _ = x_ref.shape
-    hidden = w1_ref.shape[2]
+    hidden = w1_ref.shape[1]
     row_block, col_block = out_ref.shape[1], out_ref.shape[2]
     depth = n * seqs
     pairs = seqs // 2
     me = lax.axis_index("row")
     col = lax.axis_index("col")
-
-    fetches = []
-    for layer in range(layers):
-        fetches.append(pltpu.make_async_copy(x_hbm.at[layer], x_ref.at[layer], in_sem.at[layer]))
-    fetches.append(pltpu.make_async_copy(wf_hbm, wf_ref, in_sem.at[layers]))
-    for fetch in fetches:
-        fetch.start()
 
     barrier = pltpu.get_barrier_semaphore()
     for step in range(1, n):
@@ -146,27 +142,59 @@
             device_id_type=pl.DeviceIdType.MESH,
         )
 
-    spread = (
-        lax.broadcasted_iota(jnp.int32, (hidden, LANES), 1) % hidden
-        == lax.broadcasted_iota(jnp.int32, (hidden, LANES), 0)
-    ).astype(jnp.bfloat16)
-    same = (
-        lax.broadcasted_iota(jnp.int32, (hidden, hidden), 1)
-        == lax.broadcasted_iota(jnp.int32, (hidden, hidden), 0)
-    ).astype(jnp.bfloat16)
+    fetches = []
+    for layer in range(layers):
+        fetches.append((x_hbm.at[layer], x_ref.at[layer]))
+    fetches += [(w1_hbm, w1_ref), (w2_hbm, w2_ref), (wf_hbm, wf_ref), (b_hbm, b_ref)]
+    fetches = [
+        pltpu.make_async_copy(source, target, in_sem.at[k])
+        for k, (source, target) in enumerate(fetches)
+    ]
+    for fetch in fetches:
+        fetch.start()
+    w1_fetch, w2_fetch, wf_fetch, b_fetch = fetches[layers:]
+
+    def send(source, target, send_sem, recv_sem, to):
+        copy = pltpu.make_async_remote_copy(
+            src_ref=source,
+            dst_ref=target,
+            send_sem=send_sem,
+            recv_sem=recv_sem,
+            device_id={"row": to},
+            device_id_type=pl.DeviceIdType.MESH,
+        )
+        copy.start()
+        copies.append(copy)
+
+    def arrived(buffer, recv_sem, layer, source):
+        pltpu.make_async_remote_copy(
+            src_ref=buffer.at[layer, source],
+            dst_ref=buffer.at[layer, source],
+            send_sem=left_ssem.at[layer, 0],
+            recv_sem=recv_sem.at[layer, source],
+            device_id={"row": source},
+            device_id_type=pl.DeviceIdType.MESH,
+        ).wait_recv()
+
+    partner = me + 1 - 2 * lax.rem(me, 2)
+    peers = [lax.rem(me + 2 * k, n) for k in range(1, n // 2)]
+    others = [lax.rem(partner + 2 * k, n) for k in range(n // 2)]
 
     copies = []
     for layer in range(layers):
         fetches[layer].wait()
-        w1_wide = dot32(w1_ref[layer], spread).astype(jnp.bfloat16)
-        w2_turned = dot32_nt(same, w2_ref[layer]).astype(jnp.bfloat16)
+        if layer == 0:
+            w1_fetch.wait()
+            w2_fetch.wait()
+        w1_wide = jnp.concatenate([w1_ref[layer]] * seqs, axis=0)
+        w2_turned = w2_ref[layer]
         lane = lax.broadcasted_iota(jnp.int32, (positions, LANES), 1)
         packed = jnp.zeros((positions, LANES), jnp.float32)
         for s in range(seqs):
             entry = standardize_features(x_ref[layer, s])
             normed[s] = entry
             group = (lane >= s * hidden) & (lane < (s + 1) * hidden)
-            packed = jnp.where(group, dot32(entry, w1_wide), packed)
+            packed = jnp.where(group, dot32_nt(entry, w1_wide), packed)
         left_send[layer] = packed.astype(jnp.bfloat16)
         mine = pl.ds(pl.multiple_of(col * col_block, col_block), col_block)
         for low in range(pairs):
@@ -181,27 +209,24 @@
         for step in range(1, n):
             to = lax.rem(me + step, n)
             their_rows = pl.ds(pl.multiple_of(to * row_block, row_block), row_block)
-            left_copy = pltpu.make_async_remote_copy(
-                src_ref=left_send.at[layer, their_rows, :],
-                dst_ref=left_got.at[layer, me],
-                send_sem=left_ssem.at[layer, step],
-                recv_sem=left_rsem.at[layer, me],
-                device_id={"row": to},
-                device_id_type=pl.DeviceIdType.MESH,
+            send(
+                left_send.at[layer, their_rows, :],
+                left_got.at[layer, me],
+                left_ssem.at[layer, step],
+                left_rsem.at[layer, me],
+                to,
             )
-            right_copy = pltpu.make_async_remote_copy(
-                src_ref=right_send.at[layer],
-                dst_ref=right_got.at[layer, me],
-                send_sem=right_ssem.at[layer, step],
-                recv_sem=right_rsem.at[layer, me],
-                device_id={"row": to},
-                device_id_type=pl.DeviceIdType.MESH,
+        for step, to in enumerate(peers + [partner]):
+            send(
+                right_send.at[layer],
+                right_got.at[layer, me],
+                right_ssem.at[layer, step],
+                right_rsem.at[layer, me],
+                to,
             )
-            left_copy.start()
-            right_copy.start()
-            copies.extend([left_copy, right_copy])
-
-    fetches[layers].wait()
+
+    wf_fetch.wait()
+    b_fetch.wait()
     for layer in range(layers):
         wide[...] = wf_ref[layer].astype(jnp.float32)
         for d in range(hidden):
@@ -212,16 +237,17 @@
     lane = lax.broadcasted_iota(jnp.int32, (row_block, LANES), 1)
     stores = []
     for layer in range(layers):
+        for step, source in enumerate(peers):
+            arrived(right_got, right_rsem, layer, source)
+            send(
+                right_got.at[layer, source],
+                right_got.at[layer, source],
+                right_ssem.at[layer, n // 2 + step],
+                right_rsem.at[layer, source],
+                partner,
+            )
         for step in range(1, n):
-            source = lax.rem(me + n - step, n)
-            pltpu.make_async_remote_copy(
-                src_ref=left_got.at[layer, source],
-                dst_ref=left_got.at[layer, source],
-                send_sem=left_ssem.at[layer, step],
-                recv_sem=left_rsem.at[layer, source],
-                device_id={"row": source},
-                device_id_type=pl.DeviceIdType.MESH,
-            ).wait_recv()
+            arrived(left_got, left_rsem, layer, lax.rem(me + n - step, n))
         for r in range(n):
             block = left_got[layer, r].astype(jnp.float32)
             for s in range(seqs):
@@ -236,19 +262,12 @@
             for k in range(2):
                 for i in range(row_block):
                     half_done[
-                        (d + k) * depth : (d + k + 1) * depth, i * LANES : (i + 1) * LANES
+                        layer, (d + k) * depth : (d + k + 1) * depth, i * LANES : (i + 1) * LANES
                     ] = two[i * depth : (i + 1) * depth, k * LANES : (k + 1) * LANES]
 
-        for step in range(1, n):
-            source = lax.rem(me + n - step, n)
-            pltpu.make_async_remote_copy(
-                src_ref=right_got.at[layer, source],
-                dst_ref=right_got.at[layer, source],
-                send_sem=right_ssem.at[layer, step],
-                recv_sem=right_rsem.at[layer, source],
-                device_id={"row": source},
-                device_id_type=pl.DeviceIdType.MESH,
-            ).wait_recv()
+    for layer in range(layers):
+        for source in others:
+            arrived(right_got, right_rsem, layer, source)
         for r in range(n):
             for low in range(pairs):
                 block = right_got[layer, r, low * hidden : (low + 1) * hidden, :]
@@ -260,7 +279,7 @@
         right_all = right_rows[...].T[:col_block].astype(jnp.bfloat16)
         scale = 1.0 / depth
         for i in range(0, row_block, 2):
-            two = dot32(right_all, half_done[:, i * LANES : (i + 2) * LANES]) * scale
+            two = dot32(right_all, half_done[layer, :, i * LANES : (i + 2) * LANES]) * scale
             for k in range(2):
                 done = two[:, k * LANES : (k + 1) * LANES] + b_ref[layer : layer + 1, :]
                 out_ref[layer, i + k] = done.astype(jnp.bfloat16)
@@ -278,7 +297,8 @@
     layers, seqs, positions, features = x_shape
     row_block, col_block = positions // n, positions // cols
     depth = n * seqs
-    need = 4 * layers * seqs * positions * features + 4 * depth * hidden * row_block * pair_width
+    need = layers * 4 * seqs * positions * features
+    need += layers * 4 * depth * hidden * row_block * pair_width
     return (
         seqs * hidden == LANES
         and seqs % 2 == 0
@@ -287,6 +307,7 @@
         and row_block % 16 == 0
         and depth % 16 == 0
         and n > 1
+        and n % 2 == 0
         and need < VMEM_BUDGET
     )
 
@@ -299,17 +320,19 @@
     depth = n * seqs
     packed = (seqs // 2) * hidden
     bf16, f32 = jnp.bfloat16, jnp.float32
-    vmem = pl.BlockSpec(memory_space=pltpu.VMEM)
-    anywhere = pl.BlockSpec(memory_space=pl.ANY)
+    hbm = pl.BlockSpec(memory_space=pltpu.HBM)
     out_shape = (layers, row_block, col_block, pair_width)
     return pl.pallas_call(
         functools.partial(opm_kernel, n),
         out_shape=jax.ShapeDtypeStruct(out_shape, bf16),
-        in_specs=[anywhere, vmem, vmem, anywhere, vmem],
-        out_specs=anywhere,
+        in_specs=[hbm] * 5,
+        out_specs=hbm,
         scratch_shapes=[
             pltpu.VMEM(x.shape, bf16),
+            pltpu.VMEM((layers, hidden, features), bf16),
+            pltpu.VMEM((layers, hidden, features), bf16),
             pltpu.VMEM(wf.shape, bf16),
+            pltpu.VMEM(b.shape, f32),
             pltpu.VMEM((seqs, positions, features), bf16),
             pltpu.VMEM((layers, positions, LANES), bf16),
             pltpu.VMEM((layers, packed, LANES), bf16),
@@ -319,9 +342,9 @@
             pltpu.VMEM((layers, LANES, hidden * pair_width), bf16),
             pltpu.VMEM((row_block * depth, LANES), f32),
             pltpu.VMEM((hidden * depth, LANES), f32),
-            pltpu.VMEM((hidden * depth, row_block * pair_width), bf16),
+            pltpu.VMEM((layers, hidden * depth, row_block * pair_width), bf16),
             pltpu.VMEM(out_shape, bf16),
-            pltpu.SemaphoreType.DMA((layers + 1,)),
+            pltpu.SemaphoreType.DMA((layers + 4,)),
             pltpu.SemaphoreType.DMA((layers,)),
             pltpu.SemaphoreType.DMA((layers, n)),
             pltpu.SemaphoreType.DMA((layers, n)),
@@ -332,7 +355,7 @@
             collective_id=0, has_side_effects=True, vmem_limit_bytes=VMEM_BUDGET
         ),
         name="outer_product_mean",
-    )(x, w1, w2, wf, b)
+    )(x, jnp.swapaxes(w1, 1, 2), jnp.swapaxes(w2, 1, 2), wf, b)
 
 
 def solution(mesh):

time: 20.9 us -> 19 us (0.909)
  local copies, waits for them, and re-layouts: 4.44 us -> 1.87 us
  Pallas kernels: 16.1 us -> 17 us
    unnamed x11 -> x1, local copies, waits for them, and re-layouts: 4.44 us -> 1.87 us
    pallas_call x1, Pallas kernels: 16.1 us -> 17 us  [kernel_body(): pl.pallas_call(functools.partial(opm_kernel, n), out_shape=jax.ShapeDtype...]
where the time goes in v2:
time: 19 us; the launch traced here: 18.8 us
  Pallas kernels  17 us (89%)
  local copies, waits for them, and re-layouts  1.87 us (10%)
    pallas_call x1, Pallas kernels, kernel_body(): pl.pallas_call(functools.partial(opm_kernel, n), out_shape=jax.ShapeDtype...  17 us
    unnamed x1, local copies, waits for them, and re-layouts  1.87 us

profile of v2, /device:TPU:0, one launch (start us, length us, event | category | flops | bytes accessed | tf_op | source)
XLA Modules:
  0.0 18.8 jit_solution(11803791327783823341)
XLA Ops:
  0.0 17.0 %outer_product_mean.1 = bf16[2,16,64,128]{3,2,1,0:T(8,128)(2,1)} custom-call(bf16[2,4,128,256]{3,2,1,0:T(8,128)(2,1)} %x_hbm.1, bf16[2,32,256]{2,1,0:T(8,128)(2,1)} %bitcast.2, bf16[2,32,256]{2,1,0:T(8,128)(2,1)} %bitcast.3, bf16[2,1024,128]{2,1,0:T(8,128)(2,1)} %wf_hbm.1, f32[2,128]{1,0:T(2,128)} %b_hbm.1), custom_call_target="tpu_custom_call" | custom-call | tf_op jit(solution)/shard_map/outer_product_mean/pallas_call | solution.py:325
  17.0 1.9 %copy.7 = bf16[2,16,64,128]{3,2,1,0:T(8,128)(2,1)} copy(bf16[2,16,64,128]{3,2,1,0:T(8,128)(2,1)} %outer_product_mean.1) | data formatting | bytes 1048576

commit v3 on v2

--- a/solution.py
+++ b/solution.py
@@ -117,6 +117,7 @@
     left_rows,
     right_rows,
     half_done,
+    near,
     out_ref,
     in_sem,
     out_sem,
@@ -129,6 +130,7 @@
     hidden = w1_ref.shape[1]
     row_block, col_block = out_ref.shape[1], out_ref.shape[2]
     depth = n * seqs
+    half = depth // 2
     pairs = seqs // 2
     me = lax.axis_index("row")
     col = lax.axis_index("col")
@@ -248,8 +250,8 @@
             )
         for step in range(1, n):
             arrived(left_got, left_rsem, layer, lax.rem(me + n - step, n))
-        for r in range(n):
-            block = left_got[layer, r].astype(jnp.float32)
+        for r, source in enumerate([me] + peers + others):
+            block = left_got[layer, source].astype(jnp.float32)
             for s in range(seqs):
                 group = (lane >= s * hidden) & (lane < (s + 1) * hidden)
                 left_rows[pl.ds(r * seqs + s, row_block, stride=depth), :] = jnp.where(
@@ -257,29 +259,46 @@
                 )
         left_all = left_rows[...].astype(jnp.bfloat16)
         for d in range(0, hidden, 2):
-            two = dot32(left_all, w_rows[layer, :, d * LANES : (d + 2) * LANES])
-            two = two.astype(jnp.bfloat16)
-            for k in range(2):
-                for i in range(row_block):
-                    half_done[
-                        layer, (d + k) * depth : (d + k + 1) * depth, i * LANES : (i + 1) * LANES
-                    ] = two[i * depth : (i + 1) * depth, k * LANES : (k + 1) * LANES]
-
+            weights = w_rows[layer, :, d * LANES : (d + 2) * LANES]
+            for first in range(0, row_block, 4):
+                rows = left_all[first * depth : (first + 4) * depth]
+                two = dot32(rows, weights).astype(jnp.bfloat16)
+                for k in range(2):
+                    for i in range(4):
+                        for g in range(2):
+                            at = (g * hidden + d + k) * half
+                            half_done[
+                                layer, at : at + half, (first + i) * LANES : (first + i + 1) * LANES
+                            ] = two[
+                                i * depth + g * half : i * depth + (g + 1) * half,
+                                k * LANES : (k + 1) * LANES,
+                            ]
+
+    def right_side(layer, sources):
+        for r, source in enumerate(sources):
+            for low in range(pairs):
+                block = right_got[layer, source, low * hidden : (low + 1) * hidden, :]
+                block = block.astype(jnp.float32)
+                right_rows[pl.ds(r * seqs + low, hidden, stride=half), :] = block
+                right_rows[pl.ds(r * seqs + low + pairs, hidden, stride=half), :] = pltpu.roll(
+                    block, col_block, 1
+                )
+        return right_rows[...].T[:col_block].astype(jnp.bfloat16)
+
+    for layer in range(layers):
+        right_near = right_side(layer, [me] + peers)
+        for i in range(0, row_block, 2):
+            lanes = slice(i * LANES, (i + 2) * LANES)
+            near[layer, :, lanes] = dot32(right_near, half_done[layer, : hidden * half, lanes])
+    scale = 1.0 / depth
     for layer in range(layers):
         for source in others:
             arrived(right_got, right_rsem, layer, source)
-        for r in range(n):
-            for low in range(pairs):
-                block = right_got[layer, r, low * hidden : (low + 1) * hidden, :]
-                block = block.astype(jnp.float32)
-                right_rows[pl.ds(r * seqs + low, hidden, stride=depth), :] = block
-                right_rows[pl.ds(r * seqs + low + pairs, hidden, stride=depth), :] = pltpu.roll(
-                    block, col_block, 1
-                )
-        right_all = right_rows[...].T[:col_block].astype(jnp.bfloat16)
-        scale = 1.0 / depth
+        right_far = right_side(layer, others)
         for i in range(0, row_block, 2):
-            two = dot32(right_all, half_done[layer, :, i * LANES : (i + 2) * LANES]) * scale
+            lanes = slice(i * LANES, (i + 2) * LANES)
+            two = dot32(right_far, half_done[layer, hidden * half :, lanes])
+            two = (two + near[layer, :, lanes]) * scale
             for k in range(2):
                 done = two[:, k * LANES : (k + 1) * LANES] + b_ref[layer : layer + 1, :]
                 out_ref[layer, i + k] = done.astype(jnp.bfloat16)
@@ -305,7 +324,7 @@
         and 2 * col_block == LANES
         and pair_width == LANES
         and row_block % 16 == 0
-        and depth % 16 == 0
+        and depth % 32 == 0
         and n > 1
         and n % 2 == 0
         and need < VMEM_BUDGET
@@ -341,8 +360,9 @@
             pltpu.VMEM((hidden * hidden, pair_width), f32),
             pltpu.VMEM((layers, LANES, hidden * pair_width), bf16),
             pltpu.VMEM((row_block * depth, LANES), f32),
-            pltpu.VMEM((hidden * depth, LANES), f32),
+            pltpu.VMEM((hidden * depth // 2, LANES), f32),
             pltpu.VMEM((layers, hidden * depth, row_block * pair_width), bf16),
+            pltpu.VMEM((layers, col_block, row_block * pair_width), f32),
             pltpu.VMEM(out_shape, bf16),
             pltpu.SemaphoreType.DMA((layers + 4,)),
             pltpu.SemaphoreType.DMA((layers,)),

time: 19 us -> 18.3 us (0.963)
  Pallas kernels: 17 us -> 16.3 us
    pallas_call x1, Pallas kernels: 17 us -> 16.3 us  [kernel_body(): pl.pallas_call(functools.partial(opm_kernel, n), out_shape=jax.ShapeDtype...]
where the time goes in v3:
time: 18.3 us; the launch traced here: 18.1 us
  Pallas kernels  16.3 us (89%)
  local copies, waits for them, and re-layouts  1.87 us (10%)
    pallas_call x1, Pallas kernels, kernel_body(): pl.pallas_call(functools.partial(opm_kernel, n), out_shape=jax.ShapeDtype...  16.3 us
    unnamed x1, local copies, waits for them, and re-layouts  1.87 us

profile of v3, /device:TPU:0, one launch (start us, length us, event | category | flops | bytes accessed | tf_op | source)
XLA Modules:
  0.0 18.1 jit_solution(12514063725061264931)
XLA Ops:
  0.0 16.3 %outer_product_mean.1 = bf16[2,16,64,128]{3,2,1,0:T(8,128)(2,1)} custom-call(bf16[2,4,128,256]{3,2,1,0:T(8,128)(2,1)} %x_hbm.1, bf16[2,32,256]{2,1,0:T(8,128)(2,1)} %bitcast.2, bf16[2,32,256]{2,1,0:T(8,128)(2,1)} %bitcast.3, bf16[2,1024,128]{2,1,0:T(8,128)(2,1)} %wf_hbm.1, f32[2,128]{1,0:T(2,128)} %b_hbm.1), custom_call_target="tpu_custom_call" | custom-call | tf_op jit(solution)/shard_map/outer_product_mean/pallas_call | solution.py:344
  16.3 1.9 %copy.7 = bf16[2,16,64,128]{3,2,1,0:T(8,128)(2,1)} copy(bf16[2,16,64,128]{3,2,1,0:T(8,128)(2,1)} %outer_product_mean.1) | data formatting | bytes 1048576

commit v4 on v3

--- a/solution.py
+++ b/solution.py
@@ -8,7 +8,7 @@
 from jax.sharding import PartitionSpec as P
 
 LANES = 128
-VMEM_BUDGET = 63 * 1024 * 1024
+VMEM_BUDGET = (64 * 1024 - 11200) * 1024
 
 
 def standardize_features(activations):
@@ -97,16 +97,11 @@
 def opm_kernel(
     n,
     x_hbm,
-    w1_hbm,
-    w2_hbm,
+    small_ref,
     wf_hbm,
-    b_hbm,
     out_hbm,
     x_ref,
-    w1_ref,
-    w2_ref,
     wf_ref,
-    b_ref,
     normed,
     left_send,
     right_send,
@@ -127,7 +122,7 @@
     right_rsem,
 ):
     layers, seqs, positions, _ = x_ref.shape
-    hidden = w1_ref.shape[1]
+    hidden = LANES // seqs
     row_block, col_block = out_ref.shape[1], out_ref.shape[2]
     depth = n * seqs
     half = depth // 2
@@ -147,14 +142,14 @@
     fetches = []
     for layer in range(layers):
         fetches.append((x_hbm.at[layer], x_ref.at[layer]))
-    fetches += [(w1_hbm, w1_ref), (w2_hbm, w2_ref), (wf_hbm, wf_ref), (b_hbm, b_ref)]
+    fetches.append((wf_hbm, wf_ref))
     fetches = [
         pltpu.make_async_copy(source, target, in_sem.at[k])
         for k, (source, target) in enumerate(fetches)
     ]
     for fetch in fetches:
         fetch.start()
-    w1_fetch, w2_fetch, wf_fetch, b_fetch = fetches[layers:]
+    wf_fetch = fetches[layers]
 
     def send(source, target, send_sem, recv_sem, to):
         copy = pltpu.make_async_remote_copy(
@@ -185,11 +180,8 @@
     copies = []
     for layer in range(layers):
         fetches[layer].wait()
-        if layer == 0:
-            w1_fetch.wait()
-            w2_fetch.wait()
-        w1_wide = jnp.concatenate([w1_ref[layer]] * seqs, axis=0)
-        w2_turned = w2_ref[layer]
+        w1_wide = jnp.concatenate([small_ref[layer, :hidden].astype(jnp.bfloat16)] * seqs, axis=0)
+        w2_turned = small_ref[layer, hidden : 2 * hidden].astype(jnp.bfloat16)
         lane = lax.broadcasted_iota(jnp.int32, (positions, LANES), 1)
         packed = jnp.zeros((positions, LANES), jnp.float32)
         for s in range(seqs):
@@ -228,7 +220,6 @@
             )
 
     wf_fetch.wait()
-    b_fetch.wait()
     for layer in range(layers):
         wide[...] = wf_ref[layer].astype(jnp.float32)
         for d in range(hidden):
@@ -300,7 +291,7 @@
             two = dot32(right_far, half_done[layer, hidden * half :, lanes])
             two = (two + near[layer, :, lanes]) * scale
             for k in range(2):
-                done = two[:, k * LANES : (k + 1) * LANES] + b_ref[layer : layer + 1, :]
+                done = two[:, k * LANES : (k + 1) * LANES] + small_ref[layer, 2 * hidden : 2 * hidden + 1, :LANES]
                 out_ref[layer, i + k] = done.astype(jnp.bfloat16)
         store = pltpu.make_async_copy(out_ref.at[layer], out_hbm.at[layer], out_sem.at[layer])
         store.start()
@@ -341,17 +332,17 @@
     bf16, f32 = jnp.bfloat16, jnp.float32
     hbm = pl.BlockSpec(memory_space=pltpu.HBM)
     out_shape = (layers, row_block, col_block, pair_width)
+    offsets = jnp.pad(b[:, None, :], ((0, 0), (0, 7), (0, features - pair_width)))
+    turned = [jnp.swapaxes(w, 1, 2).astype(f32) for w in (w1, w2)]
+    small = jnp.concatenate(turned + [offsets], axis=1)
     return pl.pallas_call(
         functools.partial(opm_kernel, n),
         out_shape=jax.ShapeDtypeStruct(out_shape, bf16),
-        in_specs=[hbm] * 5,
+        in_specs=[hbm, pl.BlockSpec(memory_space=pltpu.VMEM), hbm],
         out_specs=hbm,
         scratch_shapes=[
             pltpu.VMEM(x.shape, bf16),
-            pltpu.VMEM((layers, hidden, features), bf16),
-            pltpu.VMEM((layers, hidden, features), bf16),
             pltpu.VMEM(wf.shape, bf16),
-            pltpu.VMEM(b.shape, f32),
             pltpu.VMEM((seqs, positions, features), bf16),
             pltpu.VMEM((layers, positions, LANES), bf16),
             pltpu.VMEM((layers, packed, LANES), bf16),
@@ -364,7 +355,7 @@
             pltpu.VMEM((layers, hidden * depth, row_block * pair_width), bf16),
             pltpu.VMEM((layers, col_block, row_block * pair_width), f32),
             pltpu.VMEM(out_shape, bf16),
-            pltpu.SemaphoreType.DMA((layers + 4,)),
+            pltpu.SemaphoreType.DMA((layers + 1,)),
             pltpu.SemaphoreType.DMA((layers,)),
             pltpu.SemaphoreType.DMA((layers, n)),
             pltpu.SemaphoreType.DMA((layers, n)),
@@ -375,7 +366,7 @@
             collective_id=0, has_side_effects=True, vmem_limit_bytes=VMEM_BUDGET
         ),
         name="outer_product_mean",
-    )(x, jnp.swapaxes(w1, 1, 2), jnp.swapaxes(w2, 1, 2), wf, b)
+    )(x, small, wf)
 
 
 def solution(mesh):

time: 18.3 us -> 18.2 us (level)
  other arithmetic: 0 us -> 0.8 us
  Pallas kernels: 16.3 us -> 15.7 us
  local copies, waits for them, and re-layouts: 1.87 us -> 1.47 us
    convert_element_type x0 -> x1, other arithmetic: none -> 0.78 us  [kernel_body(): turned = [jnp.swapaxes(w, 1, 2).astype(f32) for w in (w1, w2)]]
    pallas_call x1, Pallas kernels: 16.3 us -> 15.7 us  [kernel_body(): pl.pallas_call(functools.partial(opm_kernel, n), out_shape=jax.ShapeDtype...]
    unnamed x1 -> x3, local copies, waits for them, and re-layouts: 1.87 us -> 1.47 us
where the time goes in v4:
time: 18.2 us; the launch traced here: 18 us
  Pallas kernels  15.7 us (86%)
  local copies, waits for them, and re-layouts  1.47 us (8%)
  other arithmetic  0.8 us (4%)
    pallas_call x1, Pallas kernels, kernel_body(): pl.pallas_call(functools.partial(opm_kernel, n), out_shape=jax.ShapeDtype...  15.7 us
    unnamed x3, local copies, waits for them, and re-layouts  1.47 us
    convert_element_type x1, other arithmetic, kernel_body(): turned = [jnp.swapaxes(w, 1, 2).astype(f32) for w in (w1, w2)]  0.78 us

profile of v4, /device:TPU:0, one launch (start us, length us, event | category | flops | bytes accessed | tf_op | source)
XLA Modules:
  0.0 18.0 jit_solution(17912963516375607319)
XLA Ops:
  0.0 0.8 %convert_bitcast_fusion = (f32[2,32,256]{2,1,0:T(8,128)S(1)}, f32[2,32,256]{2,1,0:T(8,128)S(1)}) fusion(bf16[2,256,32]{1,2,0:T(8,128)(2,1)} %param.7, bf16[2,256,32]{1,2,0:T(8,128)(2,1)} %param.6), kind=kLoop, calls=%fused_computation.2 | loop fusion | flops 32768 | bytes 196608 | tf_op jit(solution)/shard_map/convert_element_type | solution.py:336
  0.8 0.0 copy-start
  0.8 0.7 %copy-done = f32[2,128]{1,0:T(2,128)S(1)} copy-done((f32[2,128]{1,0:T(2,128)S(1)}, f32[2,128]{1,0:T(2,128)}, u32[]{:S(2)}) %copy-start) | copy-done | bytes 1048
  1.5 15.7 %outer_product_mean.1 = bf16[2,16,64,128]{3,2,1,0:T(8,128)(2,1)S(1)} custom-call(bf16[2,4,128,256]{3,2,1,0:T(8,128)(2,1)} %x_hbm.1, f32[2,72,256]{2,1,0:T(8,128)S(1)} %select_maximum_fusion.small_ref, bf16[2,1024,128]{2,1,0:T(8,128)(2,1)} %wf_hbm.1), custom_call_target="tpu_custom_call" | custom-call | tf_op jit(solution)/shard_map/outer_product_mean/pallas_call | solution.py:338
  17.2 0.8 %copy.7 = bf16[2,16,64,128]{3,2,1,0:T(8,128)(2,1)} copy(bf16[2,16,64,128]{3,2,1,0:T(8,128)(2,1)S(1)} %outer_product_mean.1) | data formatting | bytes 1048576
  (1 shorter events, 0.0 us)
Async XLA Ops:
  0.8 0.7 %copy-start = (f32[2,128]{1,0:T(2,128)S(1)}, f32[2,128]{1,0:T(2,128)}, u32[]{:S(2)}) copy-start(f32[2,128]{1,0:T(2,128)} %param.9) | copy-start | bytes 3076
